TPU v7x, 512 devices: a whole 4x4x16 slice. The times are simulated.
512 devices in a mesh: req: 32 (over x_hi, z), pre: 16 (over x_lo, y, core).
Axes of the slice: x: 4 (x_hi: 2, x_lo: 2; x = x_hi * 2 + x_lo), y: 4, z: 16, core: 2. Of those that a mesh axis runs over, the one named last changes fastest.
Arguments:
- queries: bfloat16 [128, 128, 576], P('req', 'pre'), may hold values from -120 to 120
- root_latent: bfloat16 [65536, 576], P('pre'), may hold values from -40 to 40
- suffix_latent: bfloat16 [128, 4096, 576], P('req', 'pre'), may hold values from -40 to 40
- suffix_length: int32 [128], P('req'), may hold values from 1 to 4096
- branch_pick: int32 [128], P('req'), may hold values from 0 to 3
Outputs:
- attended: bfloat16 [128, 128, 512], P('req', 'pre')
All inputs are finite; a program needn't handle non-finite values.
Results may differ from a plain program's by a relative error of at most 0.015.
Values may be sent and summed in bfloat16 or wider, within the bound.
A program may use at most 128 MiB of HBM per device.

v0:
```python
import jax
import jax.numpy as jnp
from jax import lax
from jax.sharding import PartitionSpec as P

LATENT = 512


score_scale = 192.0 ** (-0.5)


def combined_all(x, axis, combine):
    everything = jax.tree.map(lambda part: lax.all_gather(part, axis), x)
    initial = jax.tree.map(lambda part: part[0], everything)

    def step(k, so_far):
        return combine(so_far, jax.tree.map(lambda part: part[k], everything))

    return lax.fori_loop(1, lax.axis_size(axis), step, initial)


def combine_parts(first, second):
    top_first, total_first, numer_first = first
    top_second, total_second, numer_second = second
    joint = jnp.maximum(top_first, top_second)
    scale_first = jnp.exp(top_first - joint)
    scale_second = jnp.exp(top_second - joint)
    total = total_first * scale_first + total_second * scale_second
    numer = numer_first * scale_first[..., None] + numer_second * scale_second[..., None]
    return (joint, total, numer)


def local(queries, root_latent, suffix_latent, suffix_length, branch_pick):
    gathered = lax.all_gather(queries, "pre", axis=1, tiled=True)
    req_here = gathered.shape[0]
    all_heads = gathered.shape[1]
    heads_here = queries.shape[1]
    query_rows = gathered.reshape(req_here * all_heads, gathered.shape[2])
    root_scores = lax.dot_general(
        query_rows, root_latent, (((1,), (1,)), ((), ())), preferred_element_type=jnp.float32
    )
    root_scores = (root_scores * score_scale).reshape(req_here, all_heads, root_latent.shape[0])
    chosen = jnp.take(suffix_latent, branch_pick, axis=0)
    lengths = jnp.take(suffix_length, branch_pick)
    rows_here = suffix_latent.shape[1]
    position = lax.axis_index("pre") * rows_here + jnp.arange(rows_here, dtype=jnp.int32)
    valid = (position[None, :] < lengths[:, None])[:, None, :]
    suffix_scores = (
        jnp.einsum("rhc,rsc->rhs", gathered, chosen, preferred_element_type=jnp.float32)
        * score_scale
    )
    suffix_scores = jnp.where(valid, suffix_scores, -jnp.inf)
    top = jnp.maximum(jnp.max(root_scores, axis=2), jnp.max(suffix_scores, axis=2))
    root_weights = jnp.exp(root_scores - top[..., None])
    suffix_weights = jnp.where(valid, jnp.exp(suffix_scores - top[..., None]), 0.0)
    total = jnp.sum(root_weights, axis=2) + jnp.sum(suffix_weights, axis=2)
    numer = jnp.einsum(
        "rht,tc->rhc",
        root_weights.astype(jnp.bfloat16),
        root_latent[:, :LATENT],
        preferred_element_type=jnp.float32,
    )
    numer = numer + jnp.einsum(
        "rhs,rsc->rhc",
        suffix_weights.astype(jnp.bfloat16),
        chosen[:, :, :LATENT],
        preferred_element_type=jnp.float32,
    )
    joint, whole_total, whole_numer = combined_all((top, total, numer), "pre", combine_parts)
    start = lax.axis_index("pre") * heads_here
    own_total = lax.dynamic_slice_in_dim(whole_total, start, heads_here, 1)
    own_numer = lax.dynamic_slice_in_dim(whole_numer, start, heads_here, 1)
    return (own_numer / own_total[..., None]).astype(jnp.bfloat16)


def solution(mesh):
    return jax.shard_map(
        local,
        mesh=mesh,
        in_specs=(P("req", "pre", None), P("pre", None), P("req", "pre", None), P("req"), P("req")),
        out_specs=P("req", "pre", None),
        check_vma=False,
    )
```

profile of v0, /device:TPU:1, one launch (start us, length us, event | category | flops | bytes accessed | tf_op | source)
XLA Modules:
  0.0 181.0 jit_solution(5654171885392097916)
XLA Ops:
  6.5 0.8 compare_select_fusion
  7.3 1.3 gather_fusion
  8.6 0.7 broadcast_select_fusion.1
  9.3 25.1 %all_gather.17 = bf16[4,128,576]{2,1,0:T(8,128)(2,1)S(1)} all-gather(bf16[4,8,576]{2,1,0:T(8,128)(2,1)} %param.7), channel_id=1, replica_groups=mesh['req'=32,'pre'=16] {'pre'}, dimensions={1}, use_global_device_ids=true | all-gather | bytes 626688 | tf_op jit(solution)/shard_map/all_gather | solution.py:34
  35.0 1.4 copy.13
  36.5 1.5 broadcast_select_fusion
  38.6 5.8 %fusion.19 = (f32[512]{0:T(512)S(1)}, f32[512,4096]{1,0:T(8,128)S(1)}) fusion(bf16[512,576]{1,0:T(8,128)(2,1)S(1)} %bitcast.49, bf16[4096,576]{0,1:T(8,128)(2,1)} %param.8), kind=kOutput, calls=%fused_computation.45 | convolution fusion | flops 2420112896 | bytes 13699072 | tf_op jit(solution)/shard_map/dot_general | solution.py:39
  44.4 2.4 %fusion.3 = f32[4,128,512]{2,1,0:T(8,128)S(1)} fusion(f32[4,128,4096]{2,1,0:T(8,128)S(1)} %bitcast.48, bf16[4096,576]{0,1:T(8,128)(2,1)S(1)} %bitcast.52, f32[4,128]{1,0:T(4,128)S(1)} %bitcast_maximum_fusion.1), kind=kOutput, calls=%fused_computation.13 | convolution fusion | flops 2151677952 | bytes 13633536 | tf_op jit(solution)/shard_map/rht,tc->rhc/dot_general | solution.py:57
  46.8 0.8 copy-done.1
  47.6 1.6 convolution_add_fusion
  49.4 4.6 %exponential_reduce_fusion = f32[512]{0:T(512)S(1)} fusion(f32[512,4096]{1,0:T(8,128)} %copy-done.1, f32[512]{0:T(512)S(1)} %bitcast_maximum_fusion.2), kind=kLoop, calls=%fused_computation.11 | loop fusion | flops 4193792 | bytes 8392704 | tf_op jit(solution)/shard_map/reduce_sum | solution.py:56
  54.1 17.6 %all_gather.19 = f32[16,4,128]{2,1,0:T(4,128)S(1)} all-gather(f32[1,4,128]{2,1,0:T(4,128)S(1)} %bitcast_add_fusion), channel_id=1, replica_groups=mesh['req'=32,'pre'=16] {'pre'}, dimensions={0}, use_global_device_ids=true | all-gather | bytes 34816 | tf_op jit(solution)/shard_map/all_gather | solution.py:13
  71.6 16.5 %all_gather.18 = f32[16,4,128]{2,1,0:T(4,128)S(1)} all-gather(f32[1,4,128]{2,1,0:T(4,128)S(1)} %bitcast_maximum_fusion.3), channel_id=1, replica_groups=mesh['req'=32,'pre'=16] {'pre'}, dimensions={0}, use_global_device_ids=true | all-gather | bytes 34816 | tf_op jit(solution)/shard_map/all_gather | solution.py:13
  88.1 60.3 %all-gather.3.cloned.1.call-done = f32[64,128,512]{2,1,0:T(8,128)} async-done(((f32[4,128,512]{2,1,0:T(8,128)}), f32[64,128,512]{2,1,0:T(8,128)}) %all-gather.3.cloned.1.call-update) | async-done | bytes 16777232 | tf_op jit(solution)/shard_map/all_gather | solution.py:13
  148.4 1.3 slice.28
  149.7 23.6 %while.19 = (s32[]{:T(128)}, f32[4,128]{1,0:T(4,128)S(1)}, f32[4,128]{1,0:T(4,128)S(1)}, f32[4,128,512]{2,1,0:T(8,128)S(1)}, f32[16,4,128]{2,1,0:T(4,128)S(1)}, ...) while((s32[]{:T(128)}, f32[4,128]{1,0:T(4,128)S(1)}, ...), condition=%wide.region_5.6_spmd, body=%wide.region_4.5_spmd.sunk | while | flops 789509 | bytes 3166351 | solution.py:19
  149.7 1.5 fusion.27
  151.3 1.5 fusion.27
  152.9 1.5 fusion.27
  154.5 1.5 fusion.27
  156.0 1.5 fusion.27
  157.6 1.5 fusion.27
  159.2 1.5 fusion.27
  160.8 1.5 fusion.27
  162.3 1.5 fusion.27
  163.9 1.5 fusion.27
  165.5 1.5 fusion.27
  167.1 1.5 fusion.27
  168.6 1.5 fusion.27
  170.2 1.5 fusion.27
  171.8 1.5 fusion.27
  173.4 0.7 divide_convert_fusion
  (38 shorter events, 2.0 us)
Async XLA Ops:
  6.5 27.8 %copy-start = (bf16[4,256,576]{1,2,0:T(8,128)(2,1)S(1)}, bf16[4,256,576]{1,2,0:T(8,128)(2,1)}, u32[]{:S(2)}) copy-start(bf16[4,256,576]{1,2,0:T(8,128)(2,1)} %param.9) | copy-start | bytes 3538948
  6.5 141.9 %all-gather.3.cloned.1.call-start = ((), (), s32[]{:S(2)}) async-start(), calls=%async_computation | async-start | bytes 17825792 | tf_op jit(solution)/shard_map/all_gather | solution.py:13
  38.0 6.4 %slice-start = ((s8[4718592]{0:T(1024)(128)(4,1)}), s8[4194304]{0:T(1024)(128)(4,1)S(1)}, s32[]{:S(2)}) async-start(s8[4718592]{0:T(1024)(128)(4,1)} %bitcast.51), calls=%async_computation.1 | async-start | bytes 8388608
  38.6 5.8 %slice-start.1 = ((s8[4718592]{0:T(1024)(128)(4,1)}), s8[524288]{0:T(1024)(128)(4,1)S(1)}, s32[]{:S(2)}) async-start(s8[4718592]{0:T(1024)(128)(4,1)} %bitcast.51), calls=%async_computation.2 | async-start | bytes 1048576
  44.3 3.2 %copy-start.1 = (f32[512,4096]{1,0:T(8,128)}, f32[512,4096]{1,0:T(8,128)S(1)}, u32[]{:S(2)}) copy-start(f32[512,4096]{1,0:T(8,128)S(1)} %get-tuple-element.207) | copy-start | bytes 25165828
Sparse Core Ops, SparseCore 0:
  49.3 99.0 all-gather.2
where the time goes:
time: 182 us; the launch traced here: 181 us
  waiting for transfers between devices  60.3 us (33%)
  blocking collectives  59.1 us (32%)
  other arithmetic  31.8 us (17%)
  between operations  13.5 us (7%)
  matrix products  10.3 us (6%)
  local copies, waits for them, and re-layouts  5.53 us (3%)
    all_gather x1, waiting for transfers between devices, combined_all(): everything = jax.tree.map(lambda part: lax.all_gather(part, axis), x)  60.3 us
    all_gather x2, blocking collectives, combined_all(): everything = jax.tree.map(lambda part: lax.all_gather(part, axis), x)  34.1 us
    all_gather x1, blocking collectives, local(): gathered = lax.all_gather(queries, 'pre', axis=1, tiled=True)  25.1 us
    add x15, other arithmetic, combine_parts(): numer_first * scale_first[..., None]  22.8 us
    dot_general x1, matrix products, local(): lax.dot_general(query_rows, root_latent, (((1,), (1,)), ((), ())), prefer...  5.77 us
    reduce_sum x2, other arithmetic, local(): total = jnp.sum(root_weights, axis=2) + jnp.sum(suffix_weights, axis=2)  4.84 us
  transfers between devices with their start and end apart: 1, of which 1 were waited for; matrix products, arithmetic and copies ran while one was open for 3% of the time, Pallas kernels for 0%

commit v1 on v0

v1 whole, which is shorter than its diff:
```python
import functools

import jax
import jax.numpy as jnp
from jax import lax
from jax.experimental import pallas as pl
from jax.experimental.pallas import tpu as pltpu
from jax.sharding import PartitionSpec as P

MESH = pl.DeviceIdType.MESH
LATENT = 512
SCORE_SCALE = 192.0 ** (-0.5)
EXP2_SCALE = SCORE_SCALE * 1.4426950408889634
YS, XS = 4, 2
CHIPS = XS * YS
PEERS = [(dx, dy) for dx in range(XS) for dy in range(YS) if (dx, dy) != (0, 0)]
BLOCK = 512
ROOT_PARTS = 4


def kernel(
    q_hbm,
    root_hbm,
    suffix_hbm,
    lengths,
    picks,
    o_ref,
    root,
    suffix,
    near,
    far,
    scores,
    suffix_scores,
    pair_out,
    pair_top,
    pair_sum,
    got_out,
    got_top,
    got_sum,
    part_out,
    part_stat,
    all_out,
    all_stat,
    load_sem,
    ask_send,
    ask_recv,
    fwd_send,
    fwd_recv,
    pair_send,
    pair_recv,
    out_send,
    out_recv,
    stat_send,
    stat_recv,
):
    me = lax.axis_index("pre")
    core = me % 2
    chip = me // 2
    x, y = chip // YS, chip % YS
    sibling = me + 1 - 2 * core
    reqs = lengths.shape[0]
    rows = q_hbm.shape[0]
    heads = rows // reqs
    many = CHIPS * rows
    positions = root_hbm.shape[1]
    tail = suffix_hbm.shape[2]

    def target(peer):
        dx, dy = peer
        return (((x + dx) % XS) * YS + (y + dy) % YS) * 2 + core

    def source_chip(peer):
        dx, dy = peer
        return ((x + dx) % XS) * YS + (y + YS - dy) % YS

    barrier = pltpu.get_barrier_semaphore()
    for peer in PEERS:
        pl.semaphore_signal(barrier, inc=1, device_id={"pre": target(peer)}, device_id_type=MESH)
    pl.semaphore_signal(barrier, inc=1, device_id={"pre": sibling}, device_id_type=MESH)

    own = pltpu.make_async_copy(q_hbm, near.at[chip], load_sem.at[0])
    own.start()
    depth = root_hbm.shape[0] // ROOT_PARTS
    loads = [
        pltpu.make_async_copy(
            root_hbm.at[pl.ds(i * depth, depth)], root.at[pl.ds(i * depth, depth)], load_sem.at[2 + i]
        )
        for i in range(ROOT_PARTS)
    ]
    loads.append(pltpu.make_async_copy(suffix_hbm, suffix, load_sem.at[1]))
    for load in loads:
        load.start()
    own.wait()
    pl.semaphore_wait(barrier, len(PEERS) + 1)

    def remote(src, dst, send, recv, device):
        return pltpu.make_async_remote_copy(
            src_ref=src,
            dst_ref=dst,
            send_sem=send,
            recv_sem=recv,
            device_id={"pre": device},
            device_id_type=MESH,
        )

    asks = [
        remote(near.at[chip], near.at[chip], ask_send.at[i], ask_recv.at[i], target(peer))
        for i, peer in enumerate(PEERS)
    ]
    for ask in asks:
        ask.start()
    passes = [remote(near.at[chip], far.at[chip], fwd_send.at[7], fwd_recv.at[7], sibling)]
    passes[0].start()
    for load in loads:
        load.wait()
    for i, peer in enumerate(PEERS):
        asks[i].wait_recv()
        held = source_chip(peer)
        forward = remote(near.at[held], far.at[held], fwd_send.at[i], fwd_recv.at[i], sibling)
        forward.start()
        passes.append(forward)
    for forward in passes:
        forward.wait_recv()

    def score_pass(asked):
        query = asked[...].reshape(many, asked.shape[2])
        high = jnp.full((many, 128), -jnp.inf, jnp.float32)
        for j in range(positions // BLOCK):
            part = jnp.dot(
                query, root[:, j * BLOCK : (j + 1) * BLOCK], preferred_element_type=jnp.float32
            )
            scores[:, j * BLOCK : (j + 1) * BLOCK] = part
            for k in range(BLOCK // 128):
                high = jnp.maximum(high, part[:, k * 128 : (k + 1) * 128])
        wide = asked[...].astype(jnp.float32)
        place = me * tail + lax.broadcasted_iota(jnp.int32, (1, tail), 1)
        for r in range(reqs):
            mine = wide[:, r * heads : (r + 1) * heads, :]
            mine = mine.reshape(CHIPS * heads, asked.shape[2]).astype(jnp.bfloat16)
            part = jnp.dot(mine, suffix[picks[r]], preferred_element_type=jnp.float32)
            part = jnp.where(place < lengths[picks[r]], part, -jnp.inf)
            suffix_scores[:, r * heads : (r + 1) * heads, :] = part.reshape(CHIPS, heads, tail)
        whole = suffix_scores[...].reshape(many, tail)
        for k in range(tail // 128):
            high = jnp.maximum(high, whole[:, k * 128 : (k + 1) * 128])
        return jnp.max(high, axis=1, keepdims=True)

    def value_pass(top):
        lanes = jnp.zeros((many, 128), jnp.float32)
        out = jnp.zeros((many, LATENT), jnp.float32)
        for j in range(positions // BLOCK):
            weight = jnp.exp2((scores[:, j * BLOCK : (j + 1) * BLOCK] - top) * EXP2_SCALE)
            for k in range(BLOCK // 128):
                lanes = lanes + weight[:, k * 128 : (k + 1) * 128]
            out = out + lax.dot_general(
                weight.astype(jnp.bfloat16),
                root[:LATENT, j * BLOCK : (j + 1) * BLOCK],
                (((1,), (1,)), ((), ())),
                preferred_element_type=jnp.float32,
            )
        weight = jnp.exp2((suffix_scores[...].reshape(many, tail) - top) * EXP2_SCALE)
        for k in range(tail // 128):
            lanes = lanes + weight[:, k * 128 : (k + 1) * 128]
        weight = weight.reshape(CHIPS, rows, tail)
        pieces = []
        for r in range(reqs):
            mine = weight[:, r * heads : (r + 1) * heads, :]
            mine = mine.reshape(CHIPS * heads, tail).astype(jnp.bfloat16)
            part = lax.dot_general(
                mine,
                suffix[picks[r], :LATENT],
                (((1,), (1,)), ((), ())),
                preferred_element_type=jnp.float32,
            )
            pieces.append(part.reshape(CHIPS, 1, heads, LATENT))
        out = out + jnp.concatenate(pieces, axis=1).reshape(many, LATENT)
        return lanes, out

    top = score_pass(far)
    pair_top[...] = jnp.broadcast_to(top, (many, 128))
    lanes, out = value_pass(top)
    pair_sum[...] = lanes
    pair_out[...] = out.astype(jnp.bfloat16)
    pairs = [
        remote(pair_top, got_top, pair_send.at[0], pair_recv.at[0], sibling),
        remote(pair_sum, got_sum, pair_send.at[1], pair_recv.at[1], sibling),
        remote(pair_out, got_out, pair_send.at[2], pair_recv.at[2], sibling),
    ]
    for pair in pairs:
        pair.start()

    top = score_pass(near)
    for pair in pairs:
        pair.wait_recv()
    other_top = got_top[:, :1]
    joint = jnp.maximum(top, other_top)
    lanes, out = value_pass(joint)
    factor = jnp.exp2((other_top - joint) * EXP2_SCALE)
    lanes = lanes + got_sum[...] * factor
    out = out + got_out[...].astype(jnp.float32) * factor
    part_out[...] = out.astype(jnp.bfloat16).reshape(CHIPS, rows, LATENT)
    total = jnp.sum(lanes, axis=1, keepdims=True)
    row = lax.broadcasted_iota(jnp.int32, (rows, 128), 0)
    lane = lax.broadcasted_iota(jnp.int32, (rows, 128), 1)
    for j in range(CHIPS):
        here = slice(j * rows, (j + 1) * rows)
        stat = jnp.where(lane == row, joint[here], 0.0) + jnp.where(lane == row + rows, total[here], 0.0)
        part_stat[j] = jnp.sum(stat, axis=0, keepdims=True)

    sends = []
    for i, peer in enumerate(PEERS):
        device = target(peer)
        to = device // 2
        sends.append(
            remote(part_stat.at[to], all_stat.at[chip], stat_send.at[i], stat_recv.at[i], device)
        )
        sends.append(remote(part_out.at[to], all_out.at[chip], out_send.at[i], out_recv.at[i], device))
    for send in sends:
        send.start()
    all_out[chip] = part_out[chip]
    all_stat[chip] = part_stat[chip]
    for send in sends:
        send.wait_recv()

    stat = all_stat[...].reshape(CHIPS, 128)
    high = jnp.max(stat, axis=0, keepdims=True)
    share = jnp.exp2((stat - high) * EXP2_SCALE)
    sums = pltpu.roll(stat, 128 - rows, 1)
    share = share / jnp.sum(share * sums, axis=0, keepdims=True)
    result = jnp.zeros((rows, LATENT), jnp.float32)
    for j in range(CHIPS):
        column = jnp.sum(
            jnp.where(lane == row, share[j : j + 1], 0.0), axis=1, keepdims=True
        )
        result = result + all_out[j].astype(jnp.float32) * column
    o_ref[...] = result.astype(jnp.bfloat16)

    for copy in asks + passes + pairs + sends:
        copy.wait_send()


def local(queries, root_latent, suffix_latent, suffix_length, branch_pick):
    reqs, heads, width = queries.shape
    rows = reqs * heads
    positions = root_latent.shape[0]
    tail = suffix_latent.shape[1]
    many = CHIPS * rows
    count = len(PEERS)
    dma = pltpu.SemaphoreType.DMA
    out = pl.pallas_call(
        kernel,
        out_shape=jax.ShapeDtypeStruct((rows, LATENT), jnp.bfloat16),
        in_specs=[pl.BlockSpec(memory_space=pl.ANY)] * 3
        + [pl.BlockSpec(memory_space=pltpu.SMEM)] * 2,
        out_specs=pl.BlockSpec(memory_space=pltpu.VMEM),
        scratch_shapes=[
            pltpu.VMEM((width, positions), jnp.bfloat16),
            pltpu.VMEM((reqs, width, tail), jnp.bfloat16),
            pltpu.VMEM((CHIPS, rows, width), jnp.bfloat16),
            pltpu.VMEM((CHIPS, rows, width), jnp.bfloat16),
            pltpu.VMEM((many, positions), jnp.float32),
            pltpu.VMEM((CHIPS, rows, tail), jnp.float32),
            pltpu.VMEM((many, LATENT), jnp.bfloat16),
            pltpu.VMEM((many, 128), jnp.float32),
            pltpu.VMEM((many, 128), jnp.float32),
            pltpu.VMEM((many, LATENT), jnp.bfloat16),
            pltpu.VMEM((many, 128), jnp.float32),
            pltpu.VMEM((many, 128), jnp.float32),
            pltpu.VMEM((CHIPS, rows, LATENT), jnp.bfloat16),
            pltpu.VMEM((CHIPS, 1, 128), jnp.float32),
            pltpu.VMEM((CHIPS, rows, LATENT), jnp.bfloat16),
            pltpu.VMEM((CHIPS, 1, 128), jnp.float32),
            dma((2 + ROOT_PARTS,)),
            dma((count,)),
            dma((count,)),
            dma((count + 1,)),
            dma((count + 1,)),
            dma((3,)),
            dma((3,)),
            dma((count,)),
            dma((count,)),
            dma((count,)),
            dma((count,)),
        ],
        compiler_params=pltpu.CompilerParams(
            collective_id=0, has_side_effects=True, vmem_limit_bytes=56 * 2**20
        ),
    )(
        queries.reshape(rows, width),
        root_latent.T,
        suffix_latent.transpose(0, 2, 1),
        suffix_length,
        branch_pick,
    )
    return out.reshape(reqs, heads, LATENT)


def solution(mesh):
    return jax.shard_map(
        local,
        mesh=mesh,
        in_specs=(P("req", "pre", None), P("pre", None), P("req", "pre", None), P("req"), P("req")),
        out_specs=P("req", "pre", None),
        check_vma=False,
    )
```

time: 182 us -> 32.7 us (0.18)
  waiting for transfers between devices: 60.3 us -> 0 us
  blocking collectives: 59.1 us -> 0 us
  other arithmetic: 31.8 us -> 0 us
  Pallas kernels: 0 us -> 31.1 us
  between operations: 13.5 us -> 0.01 us
  matrix products: 10.3 us -> 0 us
  local copies, waits for them, and re-layouts: 5.53 us -> 1.38 us
    all_gather x1 -> x0, waiting for transfers between devices: 60.3 us -> none  [combined_all(): everything = jax.tree.map(lambda part: lax.all_gather(part, axis), x)]
    all_gather x3 -> x0, blocking collectives: 59.1 us -> none  [the longest x2 34.1 us: combined_all(): everything = jax.tree.map(lambda part: lax.all_gather(part, axis), x)]
    pallas_call x0 -> x1, Pallas kernels: none -> 31.1 us  [local(): pl.pallas_call(kernel, out_shape=jax.ShapeDtypeStruct((rows, LATENT), jnp...]
    add x32 -> x0, other arithmetic: 23.2 us -> none  [the longest x15 22.8 us: combine_parts(): numer_first * scale_first[..., None]]
    dot_general x4 -> x0, matrix products: 10.3 us -> none  [the longest x1 5.77 us: local(): lax.dot_general(query_rows, root_latent, (((1,), (1,)), ((), ())), prefer...]
    reduce_sum x2 -> x0, other arithmetic: 4.84 us -> none  [local(): total = jnp.sum(root_weights, axis=2) + jnp.sum(suffix_weights, axis=2)]
    gather x3 -> x0, local copies, waits for them, and re-layouts: 3.37 us -> none  [the longest x2 2.07 us: local(): chosen = jnp.take(suffix_latent, branch_pick, axis=0)]
    select_n x3 -> x0, other arithmetic: 2.94 us -> none  [the longest x1 1.52 us: local(): chosen = jnp.take(suffix_latent, branch_pick, axis=0)]
  transfers between devices with their start and end apart: 1 -> 0, of which waited for: 1 -> 0; matrix products, arithmetic and copies ran while one was open for 3% -> 0% of each run, Pallas kernels for 0% -> 0%
where the time goes in v1:
time: 32.7 us; the launch traced here: 32.5 us
  Pallas kernels  31.1 us (95%)
  local copies, waits for them, and re-layouts  1.38 us (4%)
    pallas_call x1, Pallas kernels, local(): pl.pallas_call(kernel, out_shape=jax.ShapeDtypeStruct((rows, LATENT), jnp...  31.1 us
    unnamed x1, local copies, waits for them, and re-layouts  1.38 us

profile of v1, /device:TPU:1, one launch (start us, length us, event | category | flops | bytes accessed | tf_op | source)
XLA Modules:
  0.0 32.5 jit_solution(8894095998169015688)
XLA Ops:
  0.0 31.1 %shard_map.55 = bf16[32,512]{1,0:T(8,128)(2,1)} custom-call(bf16[32,576]{1,0:T(8,128)(2,1)} %bitcast.7, bf16[576,4096]{1,0:T(8,128)(2,1)} %bitcast.4, bf16[4,576,256]{2,1,0:T(8,128)(2,1)} %bitcast.5, s32[4]{0:T(128)} %lengths.1, s32[4]{0:T(128)} %picks.1), custom_call_target="tpu_custom_call" | custom-call | tf_op jit(solution)/shard_map/pallas_call | solution.py:250
  31.1 1.4 %copy.7 = bf16[4,8,512]{2,1,0:T(8,128)(2,1)} copy(bf16[4,8,512]{2,1,0:T(8,128)(2,1)} %bitcast.6) | data formatting | bytes 65536

commit v2 on v1

v2 whole, which is shorter than its diff:
```python
import functools

import jax
import jax.numpy as jnp
from jax import lax
from jax.experimental import pallas as pl
from jax.experimental.pallas import tpu as pltpu
from jax.sharding import PartitionSpec as P

MESH = pl.DeviceIdType.MESH
LATENT = 512
SCORE_SCALE = 192.0 ** (-0.5)
EXP2_SCALE = SCORE_SCALE * 1.4426950408889634
YS, XS = 4, 2
CHIPS = XS * YS
PEERS = {0: (1, 0), 1: (0, 1), 2: (0, 3), 4: (1, 1), 5: (1, 3), 6: (0, 2), 7: (1, 2)}
OWN = 3
NEXT, SECOND, THIRD = (0, 1, 2), (4, 5), (6, 7)
HALF = CHIPS // 2
BLOCK = 1024
FLOOR = -1e30
ROOT_PARTS = 4


def kernel(
    q_hbm,
    root_hbm,
    suffix_hbm,
    lengths,
    picks,
    o_ref,
    keys,
    values,
    suffix,
    branch_values,
    suffix_top,
    suffix_sum,
    suffix_out,
    near,
    far,
    pair_out,
    pair_top,
    pair_sum,
    got_out,
    got_top,
    got_sum,
    part_out,
    part_stat,
    all_out,
    all_stat,
    load_sem,
    ask_send,
    ask_recv,
    fwd_send,
    fwd_recv,
    pair_send,
    pair_recv,
    out_send,
    out_recv,
    stat_send,
    stat_recv,
):
    me = lax.axis_index("pre")
    core = me % 2
    chip = me // 2
    x, y = chip // YS, chip % YS
    sibling = me + 1 - 2 * core
    reqs = lengths.shape[0]
    rows, width = q_hbm.shape
    heads = rows // reqs
    half = HALF * rows
    positions = root_hbm.shape[1]
    tail = suffix_hbm.shape[2]

    def target(peer):
        dx, dy = peer
        return (((x + dx) % XS) * YS + (y + dy) % YS) * 2 + core

    def source(peer):
        dx, dy = peer
        return (((x + dx) % XS) * YS + (y + YS - dy) % YS) * 2 + core

    barrier = pltpu.get_barrier_semaphore()
    for peer in PEERS.values():
        pl.semaphore_signal(barrier, inc=1, device_id={"pre": target(peer)}, device_id_type=MESH)
    pl.semaphore_signal(barrier, inc=1, device_id={"pre": sibling}, device_id_type=MESH)

    own = pltpu.make_async_copy(q_hbm, near.at[OWN], load_sem.at[0])
    own.start()
    depth = width // ROOT_PARTS
    loads = [
        pltpu.make_async_copy(
            root_hbm.at[pl.ds(i * depth, depth)], keys.at[pl.ds(i * depth, depth)], load_sem.at[2 + i]
        )
        for i in range(ROOT_PARTS)
    ]
    loads.append(pltpu.make_async_copy(suffix_hbm, suffix, load_sem.at[1]))
    for load in loads:
        load.start()
    own.wait()
    pl.semaphore_wait(barrier, len(PEERS) + 1)

    def remote(src, dst, send, recv, device):
        return pltpu.make_async_remote_copy(
            src_ref=src,
            dst_ref=dst,
            send_sem=send,
            recv_sem=recv,
            device_id={"pre": device},
            device_id_type=MESH,
        )

    asks = {
        i: remote(near.at[OWN], near.at[i], ask_send.at[i], ask_recv.at[i], target(peer))
        for i, peer in PEERS.items()
    }
    passes = [
        remote(near.at[i], far.at[i], fwd_send.at[i], fwd_recv.at[i], sibling) for i in range(CHIPS)
    ]

    def pass_on(i):
        asks[i].wait_recv()
        passes[i].start()

    for ask in asks.values():
        ask.start()
    passes[OWN].start()
    for load in loads:
        load.wait()

    def turn(i, carry):
        at = pl.multiple_of(i * 512, 512)
        for k in range(4):
            values[pl.ds(at + k * 128, 128), :] = keys[:LATENT, pl.ds(at + k * 128, 128)].T
        return carry

    lax.fori_loop(0, positions // 512, turn, 0)
    for r in range(reqs):
        branch_values[r] = suffix[picks[r], :LATENT].T

    place = me * tail + lax.broadcasted_iota(jnp.int32, (1, tail), 1)

    calls = []

    def lane_sums(weight):
        return sum(weight[:, k * 128 : (k + 1) * 128] for k in range(weight.shape[1] // 128))

    def joined(first, second):
        top = jnp.maximum(first[0], second[0])
        scales = [jnp.exp2((state[0] - top) * EXP2_SCALE) for state in (first, second)]
        return top, *(
            first[i].astype(jnp.float32) * scales[0] + second[i].astype(jnp.float32) * scales[1]
            for i in (1, 2)
        )

    def attend_suffix(r):
        asked = [ref[:, r * heads : (r + 1) * heads].astype(jnp.float32) for ref in (far, near)]
        asked = jnp.concatenate(asked).reshape(2 * CHIPS * heads, width).astype(jnp.bfloat16)
        part = jnp.dot(asked, suffix[picks[r]], preferred_element_type=jnp.float32)
        part = jnp.where(place < lengths[picks[r]], part, -jnp.inf)
        top = jnp.maximum(jnp.max(part, axis=1, keepdims=True), FLOOR)
        weight = jnp.exp2((part - top) * EXP2_SCALE)
        out = jnp.dot(
            weight.astype(jnp.bfloat16), branch_values[r], preferred_element_type=jnp.float32
        )
        for ref, got in (
            (suffix_top, jnp.broadcast_to(top, (top.shape[0], 128))),
            (suffix_sum, lane_sums(weight)),
            (suffix_out, out),
        ):
            ref[:, r * heads : (r + 1) * heads] = got.reshape(2 * CHIPS, heads, got.shape[1])

    def suffix_state(k):
        here = slice(k * HALF, (k + 1) * HALF)
        top, sums, out = (
            ref[here].reshape(half, ref.shape[2]) for ref in (suffix_top, suffix_sum, suffix_out)
        )
        return top[:, :1], sums, out

    def attend(asked, state, between):
        query = asked.reshape(asked.shape[0] * rows, width)

        def score(j):
            return jnp.dot(
                query, keys[:, j * BLOCK : (j + 1) * BLOCK], preferred_element_type=jnp.float32
            )

        count = positions // BLOCK
        part = score(0)
        for j in range(count):
            following = score(j + 1) if j + 1 < count else None
            high = jnp.max(part, axis=1, keepdims=True)
            if state is not None:
                high = jnp.maximum(state[0], high)
                factor = jnp.exp2((state[0] - high) * EXP2_SCALE)
            weight = jnp.exp2((part - high) * EXP2_SCALE)
            sums = lane_sums(weight)
            out = jnp.dot(
                weight.astype(jnp.bfloat16),
                values[j * BLOCK : (j + 1) * BLOCK, :],
                preferred_element_type=jnp.float32,
            )
            if state is not None:
                sums = sums + state[1] * factor
                out = out + state[2] * factor
            state, part = (high, sums, out), following
            for step in between.get(j, ()):
                step()
        return state

    pairs = {}

    def to_sibling(k, state):
        top, sums, out = state
        here = pl.ds(k * half, half)
        pair_top[here] = jnp.broadcast_to(top, (half, 128))
        pair_sum[here] = sums
        pair_out[here] = out.astype(jnp.bfloat16)
        pairs[k] = [
            remote(src.at[here], dst.at[here], pair_send.at[3 * k + i], pair_recv.at[3 * k + i], sibling)
            for i, (src, dst) in enumerate(
                ((pair_top, got_top), (pair_sum, got_sum), (pair_out, got_out))
            )
        ]
        for copy in pairs[k]:
            copy.start()

    row = lax.broadcasted_iota(jnp.int32, (rows, 128), 0)
    lane = lax.broadcasted_iota(jnp.int32, (rows, 128), 1)
    sends = []

    def to_owners(k, state):
        here = pl.ds(k * half, half)
        for copy in pairs[k]:
            copy.wait_recv()
        joint, sums, out = joined(state, (got_top[here][:, :1], got_sum[here], got_out[here]))
        out = out.astype(jnp.bfloat16)
        total = jnp.sum(sums, axis=1, keepdims=True)
        for j in reversed(range(HALF)):
            slot = k * HALF + j
            part = slice(j * rows, (j + 1) * rows)
            stat = jnp.where(lane == row, joint[part], 0.0)
            stat = stat + jnp.where(lane == row + rows, total[part], 0.0)
            stat = jnp.sum(stat, axis=0, keepdims=True)
            if slot == OWN:
                all_out[slot] = out[part]
                all_stat[slot] = stat
                continue
            part_out[slot] = out[part]
            part_stat[slot] = stat
            device = source(PEERS[slot])
            pair = [
                remote(
                    part_out.at[slot], all_out.at[slot], out_send.at[slot], out_recv.at[slot], device
                ),
                remote(
                    part_stat.at[slot], all_stat.at[slot], stat_send.at[slot], stat_recv.at[slot], device
                ),
            ]
            for copy in pair:
                copy.start()
            sends.extend(pair)

    def hook(*slots):
        return [functools.partial(pass_on, i) for i in slots]

    for i in NEXT:
        pass_on(i)
    own_first = attend(near[:HALF], None, {1: hook(*SECOND)})
    for i in (*NEXT, OWN):
        passes[i].wait_recv()
    first = attend(far[:HALF], None, {0: hook(*THIRD)})
    for i in (*SECOND, *THIRD):
        passes[i].wait_recv()
    suffixes = {j: [functools.partial(attend_suffix, j)] for j in range(reqs)}
    second = attend(far[HALF:], None, suffixes)
    to_sibling(1, joined(second, suffix_state(1)))
    to_sibling(0, joined(first, suffix_state(0)))
    own_second = attend(near[HALF:], suffix_state(3), {})
    to_owners(1, own_second)
    to_owners(0, joined(own_first, suffix_state(2)))
    for send in sends:
        send.wait_recv()

    stat = all_stat[...].reshape(CHIPS, 128)
    high = jnp.max(stat, axis=0, keepdims=True)
    share = jnp.exp2((stat - high) * EXP2_SCALE)
    totals = pltpu.roll(stat, 128 - rows, 1)
    share = share / jnp.sum(share * totals, axis=0, keepdims=True)
    result = jnp.zeros((rows, LATENT), jnp.float32)
    for j in range(CHIPS):
        column = jnp.sum(jnp.where(lane == row, share[j : j + 1], 0.0), axis=1, keepdims=True)
        result = result + all_out[j].astype(jnp.float32) * column
    o_ref[...] = result.astype(jnp.bfloat16)

    for copy in [*asks.values(), *passes, *pairs[0], *pairs[1], *sends]:
        copy.wait_send()


def local(queries, root_latent, suffix_latent, suffix_length, branch_pick):
    reqs, heads, width = queries.shape
    rows = reqs * heads
    many = CHIPS * rows
    positions = root_latent.shape[0]
    tail = suffix_latent.shape[1]
    dma = pltpu.SemaphoreType.DMA
    out = pl.pallas_call(
        kernel,
        out_shape=jax.ShapeDtypeStruct((rows, LATENT), jnp.bfloat16),
        in_specs=[pl.BlockSpec(memory_space=pl.ANY)] * 3
        + [pl.BlockSpec(memory_space=pltpu.SMEM)] * 2,
        out_specs=pl.BlockSpec(memory_space=pltpu.VMEM),
        scratch_shapes=[
            pltpu.VMEM((width, positions), jnp.bfloat16),
            pltpu.VMEM((positions, LATENT), jnp.bfloat16),
            pltpu.VMEM((reqs, width, tail), jnp.bfloat16),
            pltpu.VMEM((reqs, tail, LATENT), jnp.bfloat16),
            pltpu.VMEM((2 * CHIPS, rows, 128), jnp.float32),
            pltpu.VMEM((2 * CHIPS, rows, 128), jnp.float32),
            pltpu.VMEM((2 * CHIPS, rows, LATENT), jnp.float32),
            pltpu.VMEM((CHIPS, rows, width), jnp.bfloat16),
            pltpu.VMEM((CHIPS, rows, width), jnp.bfloat16),
            pltpu.VMEM((many, LATENT), jnp.bfloat16),
            pltpu.VMEM((many, 128), jnp.float32),
            pltpu.VMEM((many, 128), jnp.float32),
            pltpu.VMEM((many, LATENT), jnp.bfloat16),
            pltpu.VMEM((many, 128), jnp.float32),
            pltpu.VMEM((many, 128), jnp.float32),
            pltpu.VMEM((CHIPS, rows, LATENT), jnp.bfloat16),
            pltpu.VMEM((CHIPS, 1, 128), jnp.float32),
            pltpu.VMEM((CHIPS, rows, LATENT), jnp.bfloat16),
            pltpu.VMEM((CHIPS, 1, 128), jnp.float32),
            dma((2 + ROOT_PARTS,)),
            dma((CHIPS,)),
            dma((CHIPS,)),
            dma((CHIPS,)),
            dma((CHIPS,)),
            dma((6,)),
            dma((6,)),
            dma((CHIPS,)),
            dma((CHIPS,)),
            dma((CHIPS,)),
            dma((CHIPS,)),
        ],
        compiler_params=pltpu.CompilerParams(
            collective_id=0, has_side_effects=True, vmem_limit_bytes=56 * 2**20
        ),
    )(
        queries.reshape(rows, width),
        root_latent.T,
        suffix_latent.transpose(0, 2, 1),
        suffix_length,
        branch_pick,
    )
    return out.reshape(reqs, heads, LATENT)


def solution(mesh):
    return jax.shard_map(
        local,
        mesh=mesh,
        in_specs=(P("req", "pre", None), P("pre", None), P("req", "pre", None), P("req"), P("req")),
        out_specs=P("req", "pre", None),
        check_vma=False,
    )
```

time: 32.7 us -> 29.9 us (0.914)
  Pallas kernels: 31.1 us -> 28.4 us
    pallas_call x1, Pallas kernels: 31.1 us -> 28.4 us  [local(): pl.pallas_call(kernel, out_shape=jax.ShapeDtypeStruct((rows, LATENT), jnp...]
where the time goes in v2:
time: 29.9 us; the launch traced here: 29.7 us
  Pallas kernels  28.4 us (95%)
  local copies, waits for them, and re-layouts  1.38 us (5%)
    pallas_call x1, Pallas kernels, local(): pl.pallas_call(kernel, out_shape=jax.ShapeDtypeStruct((rows, LATENT), jnp...  28.4 us
    unnamed x1, local copies, waits for them, and re-layouts  1.38 us

profile of v2, /device:TPU:1, one launch (start us, length us, event | category | flops | bytes accessed | tf_op | source)
XLA Modules:
  0.0 29.7 jit_solution(7316535971297303440)
XLA Ops:
  0.0 28.4 %shard_map.55 = bf16[32,512]{1,0:T(8,128)(2,1)} custom-call(bf16[32,576]{1,0:T(8,128)(2,1)} %bitcast.7, bf16[576,4096]{1,0:T(8,128)(2,1)} %bitcast.4, bf16[4,576,256]{2,1,0:T(8,128)(2,1)} %bitcast.5, s32[4]{0:T(128)} %lengths.1, s32[4]{0:T(128)} %picks.1), custom_call_target="tpu_custom_call" | custom-call | tf_op jit(solution)/shard_map/pallas_call | solution.py:307
  28.4 1.4 %copy.7 = bf16[4,8,512]{2,1,0:T(8,128)(2,1)} copy(bf16[4,8,512]{2,1,0:T(8,128)(2,1)} %bitcast.6) | data formatting | bytes 65536

commit v3 on v2

v3 whole, which is shorter than its diff:
```python
import functools

import jax
import jax.numpy as jnp
from jax import lax
from jax.experimental import pallas as pl
from jax.experimental.pallas import tpu as pltpu
from jax.sharding import PartitionSpec as P

MESH = pl.DeviceIdType.MESH
LATENT = 512
SCORE_SCALE = 192.0 ** (-0.5)
EXP2_SCALE = SCORE_SCALE * 1.4426950408889634
YS, XS = 4, 2
CHIPS = XS * YS
PEERS = {0: (1, 0), 1: (0, 1), 2: (0, 3), 4: (1, 1), 5: (1, 3), 6: (0, 2), 7: (1, 2)}
OWN = 3
NEXT, SECOND, THIRD = (0, 1, 2), (4, 5), (6, 7)
HALF = CHIPS // 2
BLOCK = 1024
SUFFIX_AT = 3
ROOT_PARTS = 4


def kernel(
    q_hbm,
    root_hbm,
    suffix_hbm,
    lengths,
    picks,
    all_out,
    all_stat,
    keys,
    values,
    suffix,
    branch_values,
    near,
    far,
    part_out,
    part_stat,
    load_sem,
    ask_send,
    ask_recv,
    fwd_send,
    fwd_recv,
    out_send,
    out_recv,
    stat_send,
    stat_recv,
):
    me = lax.axis_index("pre")
    core = me % 2
    chip = me // 2
    x, y = chip // YS, chip % YS

    def other_core(device):
        return device + 1 - 2 * core

    sibling = other_core(me)
    reqs = lengths.shape[0]
    rows, width = q_hbm.shape
    heads = rows // reqs
    half = HALF * rows
    positions = root_hbm.shape[1]
    tail = suffix_hbm.shape[2]

    def target(peer):
        dx, dy = peer
        return (((x + dx) % XS) * YS + (y + dy) % YS) * 2 + core

    def source(peer):
        dx, dy = peer
        return (((x + dx) % XS) * YS + (y + YS - dy) % YS) * 2 + core

    barrier = pltpu.get_barrier_semaphore()
    partners = [*(target(peer) for peer in reversed(PEERS.values())), sibling]
    for partner in partners:
        pl.semaphore_signal(barrier, inc=1, device_id={"pre": partner}, device_id_type=MESH)

    own = pltpu.make_async_copy(q_hbm, near.at[OWN], load_sem.at[0])
    own.start()
    depth = width // ROOT_PARTS
    loads = [
        pltpu.make_async_copy(
            root_hbm.at[pl.ds(i * depth, depth)], keys.at[pl.ds(i * depth, depth)], load_sem.at[2 + i]
        )
        for i in range(ROOT_PARTS)
    ]
    loads.append(pltpu.make_async_copy(suffix_hbm, suffix, load_sem.at[1]))
    for load in loads:
        load.start()
    own.wait()
    pl.semaphore_wait(barrier, len(partners))

    def remote(src, dst, send, recv, device):
        return pltpu.make_async_remote_copy(
            src_ref=src,
            dst_ref=dst,
            send_sem=send,
            recv_sem=recv,
            device_id={"pre": device},
            device_id_type=MESH,
        )

    asks = {
        i: remote(near.at[OWN], near.at[i], ask_send.at[i], ask_recv.at[i], target(peer))
        for i, peer in PEERS.items()
    }
    passes = [
        remote(near.at[i], far.at[i], fwd_send.at[i], fwd_recv.at[i], sibling) for i in range(CHIPS)
    ]

    def pass_on(i):
        asks[i].wait_recv()
        passes[i].start()

    for ask in asks.values():
        ask.start()
    passes[OWN].start()
    for load in loads:
        load.wait()

    def turn(i, carry):
        at = pl.multiple_of(i * 512, 512)
        for k in range(4):
            values[pl.ds(at + k * 128, 128), :] = keys[:LATENT, pl.ds(at + k * 128, 128)].T
        return carry

    lax.fori_loop(0, positions // 512, turn, 0)
    for r in range(reqs):
        branch_values[r] = suffix[picks[r], :LATENT].T

    place = me * tail + lax.broadcasted_iota(jnp.int32, (1, tail), 1)

    calls = []

    def lane_sums(weight):
        return sum(weight[:, k * 128 : (k + 1) * 128] for k in range(weight.shape[1] // 128))

    def by_request(part):
        part = part.astype(jnp.float32).reshape(HALF, rows, part.shape[-1])
        return [
            part[:, r * heads : (r + 1) * heads].reshape(HALF * heads, part.shape[-1])
            for r in range(reqs)
        ]

    def by_row(parts):
        parts = [part.reshape(HALF, 1, heads, part.shape[-1]) for part in parts]
        return jnp.concatenate(parts, axis=1).reshape(half, parts[0].shape[-1])

    def attend(asked, between):
        query = asked.reshape(half, width)

        def root_score(j):
            return jnp.dot(
                query, keys[:, j * BLOCK : (j + 1) * BLOCK], preferred_element_type=jnp.float32
            )

        def root_product(j, weight):
            return jnp.dot(
                weight.astype(jnp.bfloat16),
                values[j * BLOCK : (j + 1) * BLOCK, :],
                preferred_element_type=jnp.float32,
            )

        def suffix_score():
            parts = []
            for r, mine in enumerate(by_request(asked)):
                part = jnp.dot(
                    mine.astype(jnp.bfloat16), suffix[picks[r]], preferred_element_type=jnp.float32
                )
                parts.append(jnp.where(place < lengths[picks[r]], part, -jnp.inf))
            return by_row(parts)

        def suffix_product(weight):
            return by_row(
                [
                    jnp.dot(
                        mine.astype(jnp.bfloat16), branch_values[r], preferred_element_type=jnp.float32
                    )
                    for r, mine in enumerate(by_request(weight))
                ]
            )

        steps = [
            (functools.partial(root_score, j), functools.partial(root_product, j))
            for j in range(positions // BLOCK)
        ]
        steps.insert(SUFFIX_AT, (suffix_score, suffix_product))
        part = steps[0][0]()
        state = None
        for j, (_, product) in enumerate(steps):
            following = steps[j + 1][0]() if j + 1 < len(steps) else None
            high = jnp.max(part, axis=1, keepdims=True)
            if state is not None:
                high = jnp.maximum(state[0], high)
                factor = jnp.exp2((state[0] - high) * EXP2_SCALE)
            weight = jnp.exp2((part - high) * EXP2_SCALE)
            sums, out = lane_sums(weight), product(weight)
            if state is not None:
                sums = sums + state[1] * factor
                out = out + state[2] * factor
            state, part = (high, sums, out), following
            for step in between.get(j, ()):
                step()
        return state

    row = lax.broadcasted_iota(jnp.int32, (rows, 128), 0)
    lane = lax.broadcasted_iota(jnp.int32, (rows, 128), 1)
    sends, kept = [], []

    def to_owners(near_rows, k, state):
        joint, sums, out = state
        out = out.astype(jnp.bfloat16)
        total = jnp.sum(sums, axis=1, keepdims=True)
        for j in reversed(range(HALF)):
            slot = k * HALF + j
            at = slot if near_rows else CHIPS + slot
            part = slice(j * rows, (j + 1) * rows)
            stat = jnp.where(lane == row, joint[part], 0.0)
            stat = stat + jnp.where(lane == row + rows, total[part], 0.0)
            stat = jnp.sum(stat, axis=0, keepdims=True)
            part_out[at] = out[part]
            part_stat[at] = stat
            if near_rows and slot == OWN:
                pair = [
                    pltpu.make_async_copy(part_out.at[at], all_out.at[at], load_sem.at[0]),
                    pltpu.make_async_copy(part_stat.at[at], all_stat.at[at], load_sem.at[1]),
                ]
                for copy in pair:
                    copy.start()
                kept.extend(pair)
                continue
            device = me if slot == OWN else source(PEERS[slot])
            device = device if near_rows else other_core(device)
            pair = [
                remote(part_out.at[at], all_out.at[at], out_send.at[at], out_recv.at[at], device),
                remote(part_stat.at[at], all_stat.at[at], stat_send.at[at], stat_recv.at[at], device),
            ]
            for copy in pair:
                copy.start()
            sends.extend(pair)

    def hook(*slots):
        return [functools.partial(pass_on, i) for i in slots]

    for i in NEXT:
        pass_on(i)
    state = attend(near[:HALF], {1: hook(*SECOND)})
    for i in THIRD:
        pass_on(i)
    to_owners(True, 0, state)
    state = attend(near[HALF:], {})
    for i in range(CHIPS):
        passes[i].wait_recv()
    to_owners(True, 1, state)
    state = attend(far[HALF:], {})
    to_owners(False, 1, state)
    state = attend(far[:HALF], {})
    to_owners(False, 0, state)
    for send in sends:
        send.wait_recv()
    for copy in kept:
        copy.wait()

    for copy in [*asks.values(), *passes, *sends]:
        copy.wait_send()


def combine(all_out, all_stat, o_ref):
    rows = o_ref.shape[0]
    row = lax.broadcasted_iota(jnp.int32, (rows, 128), 0)
    lane = lax.broadcasted_iota(jnp.int32, (rows, 128), 1)
    stat = all_stat[...].reshape(2 * CHIPS, 128)
    high = jnp.max(stat, axis=0, keepdims=True)
    share = jnp.exp2((stat - high) * EXP2_SCALE)
    totals = pltpu.roll(stat, 128 - rows, 1)
    share = share / jnp.sum(share * totals, axis=0, keepdims=True)
    result = jnp.zeros((rows, LATENT), jnp.float32)
    for j in range(2 * CHIPS):
        column = jnp.sum(jnp.where(lane == row, share[j : j + 1], 0.0), axis=1, keepdims=True)
        result = result + all_out[j].astype(jnp.float32) * column
    o_ref[...] = result.astype(jnp.bfloat16)


def local(queries, root_latent, suffix_latent, suffix_length, branch_pick):
    reqs, heads, width = queries.shape
    rows = reqs * heads
    positions = root_latent.shape[0]
    tail = suffix_latent.shape[1]
    dma = pltpu.SemaphoreType.DMA
    parts = pl.pallas_call(
        kernel,
        out_shape=[
            jax.ShapeDtypeStruct((2 * CHIPS, rows, LATENT), jnp.bfloat16),
            jax.ShapeDtypeStruct((2 * CHIPS, 1, 128), jnp.float32),
        ],
        in_specs=[pl.BlockSpec(memory_space=pl.ANY)] * 3
        + [pl.BlockSpec(memory_space=pltpu.SMEM)] * 2,
        out_specs=[pl.BlockSpec(memory_space=pl.ANY)] * 2,
        scratch_shapes=[
            pltpu.VMEM((width, positions), jnp.bfloat16),
            pltpu.VMEM((positions, LATENT), jnp.bfloat16),
            pltpu.VMEM((reqs, width, tail), jnp.bfloat16),
            pltpu.VMEM((reqs, tail, LATENT), jnp.bfloat16),
            pltpu.VMEM((CHIPS, rows, width), jnp.bfloat16),
            pltpu.VMEM((CHIPS, rows, width), jnp.bfloat16),
            pltpu.VMEM((2 * CHIPS, rows, LATENT), jnp.bfloat16),
            pltpu.VMEM((2 * CHIPS, 1, 128), jnp.float32),
            dma((2 + ROOT_PARTS,)),
            dma((CHIPS,)),
            dma((CHIPS,)),
            dma((CHIPS,)),
            dma((CHIPS,)),
            dma((2 * CHIPS,)),
            dma((2 * CHIPS,)),
            dma((2 * CHIPS,)),
            dma((2 * CHIPS,)),
        ],
        compiler_params=pltpu.CompilerParams(
            collective_id=0, has_side_effects=True, vmem_limit_bytes=56 * 2**20
        ),
    )(
        queries.reshape(rows, width),
        root_latent.T,
        suffix_latent.transpose(0, 2, 1),
        suffix_length,
        branch_pick,
    )
    out = pl.pallas_call(
        combine,
        out_shape=jax.ShapeDtypeStruct((rows, LATENT), jnp.bfloat16),
        in_specs=[pl.BlockSpec(memory_space=pltpu.VMEM)] * 2,
        out_specs=pl.BlockSpec(memory_space=pltpu.VMEM),
    )(*parts)
    return out.reshape(reqs, heads, LATENT)


def solution(mesh):
    return jax.shard_map(
        local,
        mesh=mesh,
        in_specs=(P("req", "pre", None), P("pre", None), P("req", "pre", None), P("req"), P("req")),
        out_specs=P("req", "pre", None),
        check_vma=False,
    )
```

time: 29.9 us -> 28.3 us (0.946)
  local copies, waits for them, and re-layouts: 1.38 us -> 0 us
  Pallas kernels: 28.4 us -> 28.1 us
    unnamed x1 -> x0, local copies, waits for them, and re-layouts: 1.38 us -> none
    pallas_call x1 -> x2, Pallas kernels: 28.4 us -> 28.1 us  [the longest x1 26.2 us: local(): pl.pallas_call(kernel, out_shape=[jax.ShapeDtypeStruct((2 * CHIPS, rows,...]
where the time goes in v3:
time: 28.3 us; the launch traced here: 28.1 us
  Pallas kernels  28.1 us (99%)
    pallas_call x1, Pallas kernels, local(): pl.pallas_call(kernel, out_shape=[jax.ShapeDtypeStruct((2 * CHIPS, rows,...  26.2 us
    pallas_call x1, Pallas kernels, local(): pl.pallas_call(combine, out_shape=jax.ShapeDtypeStruct((rows, LATENT), jn...  1.94 us

profile of v3, /device:TPU:1, one launch (start us, length us, event | category | flops | bytes accessed | tf_op | source)
XLA Modules:
  0.0 28.1 jit_solution(12934252253589665101)
XLA Ops:
  0.0 26.2 %shard_map.55 = (bf16[16,32,512]{2,1,0:T(8,128)(2,1)}, f32[16,1,128]{2,1,0:T(1,128)}) custom-call(bf16[32,576]{1,0:T(8,128)(2,1)} %bitcast.6, bf16[576,4096]{1,0:T(8,128)(2,1)} %bitcast.4, bf16[4,576,256]{2,1,0:T(8,128)(2,1)} %bitcast.5, s32[4]{0:T(128)} %lengths.1, s32[4]{0:T(128)} %picks.1), custom_call_target="tpu_custom_call" | custom-call | tf_op jit(solution)/shard_map/pallas_call | solution.py:292
  26.2 1.9 %shard_map.56 = bf16[32,512]{1,0:T(8,128)(2,1)} custom-call(bf16[16,32,512]{2,1,0:T(8,128)(2,1)} %get-tuple-element.7.all_out, f32[16,1,128]{2,1,0:T(1,128)} %get-tuple-element.8.all_stat), custom_call_target="tpu_custom_call" | custom-call | tf_op jit(solution)/shard_map/pallas_call | solution.py:330

commit v4 on v3

--- a/solution.py
+++ b/solution.py
@@ -103,11 +103,11 @@
         )
 
     asks = {
-        i: remote(near.at[OWN], near.at[i], ask_send.at[i], ask_recv.at[i], target(peer))
+        i: remote(near.at[OWN], near.at[i], ask_send, ask_recv.at[i], target(peer))
         for i, peer in PEERS.items()
     }
     passes = [
-        remote(near.at[i], far.at[i], fwd_send.at[i], fwd_recv.at[i], sibling) for i in range(CHIPS)
+        remote(near.at[i], far.at[i], fwd_send, fwd_recv, sibling) for i in range(CHIPS)
     ]
 
     def pass_on(i):
@@ -207,39 +207,37 @@
 
     row = lax.broadcasted_iota(jnp.int32, (rows, 128), 0)
     lane = lax.broadcasted_iota(jnp.int32, (rows, 128), 1)
-    sends, kept = [], []
-
-    def to_owners(near_rows, k, state):
+    kept = []
+
+    def store(near_rows, k, state):
         joint, sums, out = state
-        out = out.astype(jnp.bfloat16)
+        base = (0 if near_rows else CHIPS) + k * HALF
+        part_out[base : base + HALF] = out.astype(jnp.bfloat16).reshape(HALF, rows, LATENT)
         total = jnp.sum(sums, axis=1, keepdims=True)
-        for j in reversed(range(HALF)):
-            slot = k * HALF + j
-            at = slot if near_rows else CHIPS + slot
+        for j in range(HALF):
             part = slice(j * rows, (j + 1) * rows)
             stat = jnp.where(lane == row, joint[part], 0.0)
             stat = stat + jnp.where(lane == row + rows, total[part], 0.0)
-            stat = jnp.sum(stat, axis=0, keepdims=True)
-            part_out[at] = out[part]
-            part_stat[at] = stat
+            part_stat[base + j] = jnp.sum(stat, axis=0, keepdims=True)
+
+    def send(near_rows, k):
+        for slot in reversed(range(k * HALF, (k + 1) * HALF)):
+            at = slot if near_rows else CHIPS + slot
             if near_rows and slot == OWN:
                 pair = [
                     pltpu.make_async_copy(part_out.at[at], all_out.at[at], load_sem.at[0]),
                     pltpu.make_async_copy(part_stat.at[at], all_stat.at[at], load_sem.at[1]),
                 ]
-                for copy in pair:
-                    copy.start()
                 kept.extend(pair)
-                continue
-            device = me if slot == OWN else source(PEERS[slot])
-            device = device if near_rows else other_core(device)
-            pair = [
-                remote(part_out.at[at], all_out.at[at], out_send.at[at], out_recv.at[at], device),
-                remote(part_stat.at[at], all_stat.at[at], stat_send.at[at], stat_recv.at[at], device),
-            ]
+            else:
+                device = me if slot == OWN else source(PEERS[slot])
+                device = device if near_rows else other_core(device)
+                pair = [
+                    remote(part_out.at[at], all_out.at[at], out_send, out_recv, device),
+                    remote(part_stat.at[at], all_stat.at[at], stat_send, stat_recv, device),
+                ]
             for copy in pair:
                 copy.start()
-            sends.extend(pair)
 
     def hook(*slots):
         return [functools.partial(pass_on, i) for i in slots]
@@ -249,22 +247,30 @@
     state = attend(near[:HALF], {1: hook(*SECOND)})
     for i in THIRD:
         pass_on(i)
-    to_owners(True, 0, state)
+    store(True, 0, state)
+    send(True, 0)
     state = attend(near[HALF:], {})
-    for i in range(CHIPS):
-        passes[i].wait_recv()
-    to_owners(True, 1, state)
+    every_pass = remote(near, far, fwd_send, fwd_recv, sibling)
+    every_pass.wait_recv()
+    store(True, 1, state)
+    send(True, 1)
     state = attend(far[HALF:], {})
-    to_owners(False, 1, state)
+    store(False, 1, state)
+    send(False, 1)
     state = attend(far[:HALF], {})
-    to_owners(False, 0, state)
-    for send in sends:
-        send.wait_recv()
+    store(False, 0, state)
+    send(False, 0)
+    most = pl.ds(0, 2 * CHIPS - 1)
+    outs = remote(part_out.at[most], all_out.at[most], out_send, out_recv, sibling)
+    stats = remote(part_stat.at[most], all_stat.at[most], stat_send, stat_recv, sibling)
+    others = pl.ds(0, len(PEERS))
+    every_ask = remote(near.at[others], near.at[others], ask_send, ask_recv.at[OWN], sibling)
+    for copy in (every_ask, every_pass, outs, stats):
+        copy.wait_send()
     for copy in kept:
         copy.wait()
-
-    for copy in [*asks.values(), *passes, *sends]:
-        copy.wait_send()
+    outs.wait_recv()
+    stats.wait_recv()
 
 
 def combine(all_out, all_stat, o_ref):
@@ -308,14 +314,14 @@
             pltpu.VMEM((2 * CHIPS, rows, LATENT), jnp.bfloat16),
             pltpu.VMEM((2 * CHIPS, 1, 128), jnp.float32),
             dma((2 + ROOT_PARTS,)),
+            dma,
             dma((CHIPS,)),
-            dma((CHIPS,)),
-            dma((CHIPS,)),
-            dma((CHIPS,)),
-            dma((2 * CHIPS,)),
-            dma((2 * CHIPS,)),
-            dma((2 * CHIPS,)),
-            dma((2 * CHIPS,)),
+            dma,
+            dma,
+            dma,
+            dma,
+            dma,
+            dma,
         ],
         compiler_params=pltpu.CompilerParams(
             collective_id=0, has_side_effects=True, vmem_limit_bytes=56 * 2**20

time: 28.3 us -> 27.5 us (0.972)
  Pallas kernels: 28.1 us -> 27.3 us
    pallas_call x1, Pallas kernels: 26.2 us -> 25.4 us  [local(): pl.pallas_call(kernel, out_shape=[jax.ShapeDtypeStruct((2 * CHIPS, rows,...]
where the time goes in v4:
time: 27.5 us; the launch traced here: 27.3 us
  Pallas kernels  27.3 us (99%)
    pallas_call x1, Pallas kernels, local(): pl.pallas_call(kernel, out_shape=[jax.ShapeDtypeStruct((2 * CHIPS, rows,...  25.4 us
    pallas_call x1, Pallas kernels, local(): pl.pallas_call(combine, out_shape=jax.ShapeDtypeStruct((rows, LATENT), jn...  1.94 us

profile of v4, /device:TPU:1, one launch (start us, length us, event | category | flops | bytes accessed | tf_op | source)
XLA Modules:
  0.0 27.3 jit_solution(7373415247440883703)
XLA Ops:
  0.0 25.4 %shard_map.55 = (bf16[16,32,512]{2,1,0:T(8,128)(2,1)}, f32[16,1,128]{2,1,0:T(1,128)}) custom-call(bf16[32,576]{1,0:T(8,128)(2,1)} %bitcast.6, bf16[576,4096]{1,0:T(8,128)(2,1)} %bitcast.4, bf16[4,576,256]{2,1,0:T(8,128)(2,1)} %bitcast.5, s32[4]{0:T(128)} %lengths.1, s32[4]{0:T(128)} %picks.1), custom_call_target="tpu_custom_call" | custom-call | tf_op jit(solution)/shard_map/pallas_call | solution.py:298
  25.4 1.9 %shard_map.56 = bf16[32,512]{1,0:T(8,128)(2,1)} custom-call(bf16[16,32,512]{2,1,0:T(8,128)(2,1)} %get-tuple-element.7.all_out, f32[16,1,128]{2,1,0:T(1,128)} %get-tuple-element.8.all_stat), custom_call_target="tpu_custom_call" | custom-call | tf_op jit(solution)/shard_map/pallas_call | solution.py:336

commit v5 on v4

--- a/solution.py
+++ b/solution.py
@@ -17,8 +17,9 @@
 OWN = 3
 NEXT, SECOND, THIRD = (0, 1, 2), (4, 5), (6, 7)
 HALF = CHIPS // 2
-BLOCK = 1024
-SUFFIX_AT = 3
+BLOCK = 2048
+SUFFIX_AT = 1
+FLOOR = -1e30
 ROOT_PARTS = 4
 
 
@@ -138,72 +139,80 @@
         return sum(weight[:, k * 128 : (k + 1) * 128] for k in range(weight.shape[1] // 128))
 
     def by_request(part):
-        part = part.astype(jnp.float32).reshape(HALF, rows, part.shape[-1])
+        chips = part.shape[0]
+        part = part.astype(jnp.float32)
         return [
-            part[:, r * heads : (r + 1) * heads].reshape(HALF * heads, part.shape[-1])
+            part[:, r * heads : (r + 1) * heads].reshape(chips * heads, part.shape[2])
             for r in range(reqs)
         ]
 
     def by_row(parts):
-        parts = [part.reshape(HALF, 1, heads, part.shape[-1]) for part in parts]
-        return jnp.concatenate(parts, axis=1).reshape(half, parts[0].shape[-1])
-
-    def attend(asked, between):
+        parts = [part.reshape(-1, 1, heads, part.shape[1]) for part in parts]
+        return jnp.concatenate(parts, axis=1).reshape(-1, parts[0].shape[3])
+
+    def weigh(part, state):
+        top = jnp.max(part, axis=1, keepdims=True)
+        scale = None
+        if state is not None:
+            top = jnp.maximum(state[0], top)
+            scale = jnp.exp2((state[0] - top) * EXP2_SCALE)
+        return top, jnp.exp2((part - top) * EXP2_SCALE), scale
+
+    def grown(state, top, weight, scale, out):
+        sums = lane_sums(weight)
+        if state is not None:
+            sums, out = sums + state[1] * scale, out + state[2] * scale
+        return top, sums, out
+
+    def suffix_scores(asked):
+        parts = []
+        for r, mine in enumerate(by_request(asked)):
+            part = jnp.dot(
+                mine.astype(jnp.bfloat16), suffix[picks[r]], preferred_element_type=jnp.float32
+            )
+            parts.append(jnp.where(place < lengths[picks[r]], part, -jnp.inf))
+        return by_row(parts)
+
+    def suffix_products(weight):
+        weight = weight.reshape(-1, rows, tail)
+        return by_row(
+            [
+                jnp.dot(
+                    mine.astype(jnp.bfloat16), branch_values[r], preferred_element_type=jnp.float32
+                )
+                for r, mine in enumerate(by_request(weight))
+            ]
+        )
+
+    def attend(asked, state, between, both=None, other=None):
         query = asked.reshape(half, width)
 
-        def root_score(j):
+        def score(j):
             return jnp.dot(
                 query, keys[:, j * BLOCK : (j + 1) * BLOCK], preferred_element_type=jnp.float32
             )
 
-        def root_product(j, weight):
-            return jnp.dot(
+        count = positions // BLOCK
+        part = score(0)
+        for j in range(count):
+            following = score(j + 1) if j + 1 < count else None
+            if both is not None and j == SUFFIX_AT:
+                ends = suffix_scores(both)
+            top, weight, scale = weigh(part, state)
+            out = jnp.dot(
                 weight.astype(jnp.bfloat16),
                 values[j * BLOCK : (j + 1) * BLOCK, :],
                 preferred_element_type=jnp.float32,
             )
-
-        def suffix_score():
-            parts = []
-            for r, mine in enumerate(by_request(asked)):
-                part = jnp.dot(
-                    mine.astype(jnp.bfloat16), suffix[picks[r]], preferred_element_type=jnp.float32
-                )
-                parts.append(jnp.where(place < lengths[picks[r]], part, -jnp.inf))
-            return by_row(parts)
-
-        def suffix_product(weight):
-            return by_row(
-                [
-                    jnp.dot(
-                        mine.astype(jnp.bfloat16), branch_values[r], preferred_element_type=jnp.float32
-                    )
-                    for r, mine in enumerate(by_request(weight))
-                ]
-            )
-
-        steps = [
-            (functools.partial(root_score, j), functools.partial(root_product, j))
-            for j in range(positions // BLOCK)
-        ]
-        steps.insert(SUFFIX_AT, (suffix_score, suffix_product))
-        part = steps[0][0]()
-        state = None
-        for j, (_, product) in enumerate(steps):
-            following = steps[j + 1][0]() if j + 1 < len(steps) else None
-            high = jnp.max(part, axis=1, keepdims=True)
-            if state is not None:
-                high = jnp.maximum(state[0], high)
-                factor = jnp.exp2((state[0] - high) * EXP2_SCALE)
-            weight = jnp.exp2((part - high) * EXP2_SCALE)
-            sums, out = lane_sums(weight), product(weight)
-            if state is not None:
-                sums = sums + state[1] * factor
-                out = out + state[2] * factor
-            state, part = (high, sums, out), following
+            state, part = grown(state, top, weight, scale, out), following
+            if both is not None and j == SUFFIX_AT:
+                first, second = weigh(ends[:half], other), weigh(ends[half:], state)
+                out = suffix_products(jnp.concatenate([first[1], second[1]]))
+                other = grown(other, *first, out[:half])
+                state = grown(state, *second, out[half:])
             for step in between.get(j, ()):
                 step()
-        return state
+        return state if both is None else (other, state)
 
     row = lax.broadcasted_iota(jnp.int32, (rows, 128), 0)
     lane = lax.broadcasted_iota(jnp.int32, (rows, 128), 1)
@@ -244,21 +253,25 @@
 
     for i in NEXT:
         pass_on(i)
-    state = attend(near[:HALF], {1: hook(*SECOND)})
+    first = attend(near[:HALF], None, {0: hook(*SECOND)})
     for i in THIRD:
         pass_on(i)
-    store(True, 0, state)
+    first, second = attend(near[HALF:], None, {}, near[...], first)
+    store(True, 1, second)
+    store(True, 0, first)
+    send(True, 1)
     send(True, 0)
-    state = attend(near[HALF:], {})
     every_pass = remote(near, far, fwd_send, fwd_recv, sibling)
     every_pass.wait_recv()
-    store(True, 1, state)
-    send(True, 1)
-    state = attend(far[HALF:], {})
-    store(False, 1, state)
+    first = (
+        jnp.full((half, 1), FLOOR, jnp.float32),
+        jnp.zeros((half, 128), jnp.float32),
+        jnp.zeros((half, LATENT), jnp.float32),
+    )
+    first, second = attend(far[HALF:], None, {}, far[...], first)
+    store(False, 1, second)
     send(False, 1)
-    state = attend(far[:HALF], {})
-    store(False, 0, state)
+    store(False, 0, attend(far[:HALF], first, {}))
     send(False, 0)
     most = pl.ds(0, 2 * CHIPS - 1)
     outs = remote(part_out.at[most], all_out.at[most], out_send, out_recv, sibling)

time: 27.5 us -> 26.8 us (0.975)
  Pallas kernels: 27.3 us -> 26.6 us
    pallas_call x1, Pallas kernels: 25.4 us -> 24.7 us  [local(): pl.pallas_call(kernel, out_shape=[jax.ShapeDtypeStruct((2 * CHIPS, rows,...]
where the time goes in v5:
time: 26.8 us; the launch traced here: 26.6 us
  Pallas kernels  26.6 us (99%)
    pallas_call x1, Pallas kernels, local(): pl.pallas_call(kernel, out_shape=[jax.ShapeDtypeStruct((2 * CHIPS, rows,...  24.7 us
    pallas_call x1, Pallas kernels, local(): pl.pallas_call(combine, out_shape=jax.ShapeDtypeStruct((rows, LATENT), jn...  1.94 us

profile of v5, /device:TPU:1, one launch (start us, length us, event | category | flops | bytes accessed | tf_op | source)
XLA Modules:
  0.0 26.6 jit_solution(11119495418299532520)
XLA Ops:
  0.0 24.7 %shard_map.55 = (bf16[16,32,512]{2,1,0:T(8,128)(2,1)}, f32[16,1,128]{2,1,0:T(1,128)}) custom-call(bf16[32,576]{1,0:T(8,128)(2,1)} %bitcast.6, bf16[576,4096]{1,0:T(8,128)(2,1)} %bitcast.4, bf16[4,576,256]{2,1,0:T(8,128)(2,1)} %bitcast.5, s32[4]{0:T(128)} %lengths.1, s32[4]{0:T(128)} %picks.1), custom_call_target="tpu_custom_call" | custom-call | tf_op jit(solution)/shard_map/pallas_call | solution.py:311
  24.7 1.9 %shard_map.56 = bf16[32,512]{1,0:T(8,128)(2,1)} custom-call(bf16[16,32,512]{2,1,0:T(8,128)(2,1)} %get-tuple-element.7.all_out, f32[16,1,128]{2,1,0:T(1,128)} %get-tuple-element.8.all_stat), custom_call_target="tpu_custom_call" | custom-call | tf_op jit(solution)/shard_map/pallas_call | solution.py:349

commit v6 on v5

--- a/solution.py
+++ b/solution.py
@@ -27,10 +27,12 @@
     q_hbm,
     root_hbm,
     suffix_hbm,
+    lengths_hbm,
+    picks_hbm,
+    all_out,
+    all_stat,
     lengths,
     picks,
-    all_out,
-    all_stat,
     keys,
     values,
     suffix,
@@ -87,7 +89,11 @@
         )
         for i in range(ROOT_PARTS)
     ]
-    loads.append(pltpu.make_async_copy(suffix_hbm, suffix, load_sem.at[1]))
+    loads += [
+        pltpu.make_async_copy(suffix_hbm, suffix, load_sem.at[1]),
+        pltpu.make_async_copy(lengths_hbm, lengths, load_sem.at[2 + ROOT_PARTS]),
+        pltpu.make_async_copy(picks_hbm, picks, load_sem.at[3 + ROOT_PARTS]),
+    ]
     for load in loads:
         load.start()
     own.wait()
@@ -121,15 +127,21 @@
     for load in loads:
         load.wait()
 
-    def turn(i, carry):
-        at = pl.multiple_of(i * 512, 512)
+    def turn(at):
+        values[pl.ds(at, 128), :] = keys[:LATENT, pl.ds(at, 128)].T
+
+    def turn_some(i, carry):
         for k in range(4):
-            values[pl.ds(at + k * 128, 128), :] = keys[:LATENT, pl.ds(at + k * 128, 128)].T
+            turn(pl.multiple_of(i * 512 + k * 128, 128))
         return carry
 
-    lax.fori_loop(0, positions // 512, turn, 0)
-    for r in range(reqs):
-        branch_values[r] = suffix[picks[r], :LATENT].T
+    def turn_rest():
+        for at in range(BLOCK, positions, 128):
+            turn(at)
+        for r in range(reqs):
+            branch_values[r] = suffix[picks[r], :LATENT].T
+
+    lax.fori_loop(0, BLOCK // 512, turn_some, 0)
 
     place = me * tail + lax.broadcasted_iota(jnp.int32, (1, tail), 1)
 
@@ -188,9 +200,10 @@
         query = asked.reshape(half, width)
 
         def score(j):
+            here = slice(j * BLOCK, (j + 1) * BLOCK)
             return jnp.dot(
-                query, keys[:, j * BLOCK : (j + 1) * BLOCK], preferred_element_type=jnp.float32
-            )
+                query[:, :LATENT], keys[:LATENT, here], preferred_element_type=jnp.float32
+            ) + jnp.dot(query[:, LATENT:], keys[LATENT:, here], preferred_element_type=jnp.float32)
 
         count = positions // BLOCK
         part = score(0)
@@ -253,7 +266,7 @@
 
     for i in NEXT:
         pass_on(i)
-    first = attend(near[:HALF], None, {0: hook(*SECOND)})
+    first = attend(near[:HALF], None, {0: [turn_rest, *hook(*SECOND)]})
     for i in THIRD:
         pass_on(i)
     first, second = attend(near[HALF:], None, {}, near[...], first)
@@ -314,10 +327,11 @@
             jax.ShapeDtypeStruct((2 * CHIPS, rows, LATENT), jnp.bfloat16),
             jax.ShapeDtypeStruct((2 * CHIPS, 1, 128), jnp.float32),
         ],
-        in_specs=[pl.BlockSpec(memory_space=pl.ANY)] * 3
-        + [pl.BlockSpec(memory_space=pltpu.SMEM)] * 2,
+        in_specs=[pl.BlockSpec(memory_space=pl.ANY)] * 5,
         out_specs=[pl.BlockSpec(memory_space=pl.ANY)] * 2,
         scratch_shapes=[
+            pltpu.SMEM((reqs,), jnp.int32),
+            pltpu.SMEM((reqs,), jnp.int32),
             pltpu.VMEM((width, positions), jnp.bfloat16),
             pltpu.VMEM((positions, LATENT), jnp.bfloat16),
             pltpu.VMEM((reqs, width, tail), jnp.bfloat16),
@@ -326,7 +340,7 @@
             pltpu.VMEM((CHIPS, rows, width), jnp.bfloat16),
             pltpu.VMEM((2 * CHIPS, rows, LATENT), jnp.bfloat16),
             pltpu.VMEM((2 * CHIPS, 1, 128), jnp.float32),
-            dma((2 + ROOT_PARTS,)),
+            dma((4 + ROOT_PARTS,)),
             dma,
             dma((CHIPS,)),
             dma,

time: 26.8 us -> 26.1 us (0.974)
  Pallas kernels: 26.6 us -> 25.9 us
    pallas_call x1, Pallas kernels: 24.7 us -> 24 us  [local(): pl.pallas_call(kernel, out_shape=[jax.ShapeDtypeStruct((2 * CHIPS, rows,...]
where the time goes in v6:
time: 26.1 us; the launch traced here: 25.9 us
  Pallas kernels  25.9 us (99%)
    pallas_call x1, Pallas kernels, local(): pl.pallas_call(kernel, out_shape=[jax.ShapeDtypeStruct((2 * CHIPS, rows,...  24 us
    pallas_call x1, Pallas kernels, local(): pl.pallas_call(combine, out_shape=jax.ShapeDtypeStruct((rows, LATENT), jn...  1.94 us

profile of v6, /device:TPU:1, one launch (start us, length us, event | category | flops | bytes accessed | tf_op | source)
XLA Modules:
  0.0 25.9 jit_solution(4124121407187886296)
XLA Ops:
  0.0 24.0 %shard_map.55 = (bf16[16,32,512]{2,1,0:T(8,128)(2,1)}, f32[16,1,128]{2,1,0:T(1,128)}) custom-call(bf16[32,576]{1,0:T(8,128)(2,1)} %bitcast.6, bf16[576,4096]{1,0:T(8,128)(2,1)} %bitcast.4, bf16[4,576,256]{2,1,0:T(8,128)(2,1)} %bitcast.5, s32[4]{0:T(128)} %lengths_hbm.1, s32[4]{0:T(128)} %picks_hbm.1), custom_call_target="tpu_custom_call" | custom-call | tf_op jit(solution)/shard_map/pallas_call | solution.py:324
  24.0 1.9 %shard_map.56 = bf16[32,512]{1,0:T(8,128)(2,1)} custom-call(bf16[16,32,512]{2,1,0:T(8,128)(2,1)} %get-tuple-element.7.all_out, f32[16,1,128]{2,1,0:T(1,128)} %get-tuple-element.8.all_stat), custom_call_target="tpu_custom_call" | custom-call | tf_op jit(solution)/shard_map/pallas_call | solution.py:363
